TPU v7x, 256 devices: a whole 4x4x8 slice. The times are simulated.
256 devices in a mesh: item: 32 (over x, z), cent: 8 (over y, core).
Axes of the slice: x: 4, y: 4, z: 8, core: 2. Of those that a mesh axis runs over, the one named last changes fastest.
Arguments:
- vectors: float32 [32768, 256], P('item'), may hold values from -15 to 15, as said below
- centroids: float32 [32768, 256], P('cent'), may hold values from -15 to 15, as said below
Outputs:
- refined: float32 [32768, 256], P('cent')
- log_partition: float32 [32768], P('item')
Inputs may be any that keep to these rules, and one draw needn't show every extreme that they name: Entries of order one; a few vectors lie on or near centroids, with large norms. Entries of order one or less; a few centroids are larger.
All inputs are finite; a program needn't handle non-finite values.
Results may differ from a plain program's by a relative error of at most 0.0001.
Values sent between devices are 32-bit elements; how exact they have to be, the bound alone decides.
A program may use at most 128 MiB of HBM per device.

v0:
```python
import functools
import math

import jax
import jax.numpy as jnp
from jax import lax
from jax.experimental import pallas as pl
from jax.experimental.pallas import tpu as pltpu
from jax.sharding import PartitionSpec as P

MESH = pl.DeviceIdType.MESH
BOLTZMANN_SCALE = 8.0
PRIOR = 2.0
LOG2E = math.log2(math.e)
LN2 = math.log(2.0)
XSCALE = 2.0 * LOG2E / BOLTZMANN_SCALE

NX, NZ, NC = 4, 8, 8
D = 256
N = 1024
KP = 4096
RA, RB = 80, 48
CA, CB = NZ * RA, NX * RB
B0 = NX * CA
TB = 768
NTB = NZ * CB // TB
NT = NX + NTB
Q = 2

STAT, W1, W2, BX, GBX = range(5)
A1 = 5
A2 = A1 + 8
AZ = A2 + 8
BZ = AZ + 4
GAZ = BZ + 4 * Q
GA1 = GAZ + 4
GA2 = GA1 + 8
GBZ = GA2 + 8
NRECV = GBZ + 16
S_STAT, S_W1, S_W2, S_BX, S_GBX, S_A1, S_A2, S_AZ, S_BZ, S_GAZ, S_GA1, S_GA2, S_GBZ = range(13)
NSEND = 13

ORDER_RS = (4, 3, -3, 2, -2, 1, -1, 0)
ORDER_AG = (0, -1, 1, -2, 2, -3, 3, 4)
ORDER_T = (0, -1, 1, 2)


def dot(a, b):
    return jnp.dot(a, b, preferred_element_type=jnp.float32)


def split(v):
    hi = v.astype(jnp.bfloat16)
    lo = (v - hi.astype(jnp.float32)).astype(jnp.bfloat16)
    return hi, lo


def kernel(
    x_hbm, c_hbm, out, lse_out,
    xbuf, cbuf, xh, xl, xht, xlt, e_buf, m_buf, s_buf, f_buf, stat, numer, w8,
    wown, rw1, w2s, rw2, ra1, ra2, raz0, raz, rbz0, rbz, rbx, den,
    ss, rs, lsem,
):
    item = lax.axis_index("item")
    cent = lax.axis_index("cent")
    x, z = item // NZ, lax.rem(item, NZ)

    def mod(v, n):
        return lax.rem(v + 2 * n, n)

    def at_x(d):
        return {"item": mod(x + d, NX) * NZ + z}

    def at_z(d):
        return {"item": x * NZ + mod(z + d, NZ)}

    def at_c(d):
        return {"cent": mod(cent + d, NC)}

    def copy(src, dst, kind, k, dev):
        return pltpu.make_async_remote_copy(
            src_ref=src, dst_ref=dst, send_sem=ss.at[kind], recv_sem=rs.at[k],
            device_id=dev, device_id_type=MESH,
        )

    def send(src, dst, kind, k, dev):
        copy(src, dst, kind, k, dev).start()

    def got(region, k):
        copy(region, region, 0, k, at_x(1)).wait_recv()

    def sent(region, kind):
        copy(region, region, kind, 0, at_x(1)).wait_send()

    def x_load(j):
        rows = pl.ds(j * 256, 256)
        return pltpu.make_async_copy(x_hbm.at[rows], xbuf.at[rows], lsem.at[NT + j])

    for j in range(N // 256):
        x_load(j).start()

    def tile_rows(t, rows_n, base):
        return pl.ds(pl.multiple_of(base + t * rows_n, 8), rows_n)

    def c_load(t, rows_n, base, k):
        rows = tile_rows(t, rows_n, base)
        return pltpu.make_async_copy(c_hbm.at[rows], cbuf.at[rows], lsem.at[k])

    for t in range(NX):
        c_load(t, CA, 0, t).start()
    for t in range(NTB):
        c_load(t, TB, B0, NX + t).start()

    barrier = pltpu.get_barrier_semaphore()
    for d in range(1, NX):
        pl.semaphore_signal(barrier, inc=1, device_id=at_x(d), device_id_type=MESH)
    for d in range(1, NZ):
        pl.semaphore_signal(barrier, inc=1, device_id=at_z(d), device_id_type=MESH)
    for d in range(1, NC):
        pl.semaphore_signal(barrier, inc=1, device_id=at_c(d), device_id_type=MESH)

    for j in range(N // 256):
        x_load(j).wait()
        rows = pl.ds(j * 256, 256)
        v = xbuf[rows, :] * XSCALE
        hi, lo = split(v)
        xh[rows, :] = hi
        xl[rows, :] = lo
        hi, lo = split(v.T)
        xht[:, rows] = hi
        xlt[:, rows] = lo

    def stage_a(rows_n, base, first):
        def tile(t, _):
            c_load(t, rows_n, base, first + t).wait()
            rows = tile_rows(t, rows_n, base)
            c = cbuf[rows, :]
            csq = jnp.sum(c * c, axis=1, keepdims=True) * (LOG2E / BOLTZMANN_SCALE)
            ch, cl = split(c)
            for j in range(N // 256):
                cols = pl.ds(j * 256, 256)
                b = xht[:, cols]
                l = dot(ch, b) + dot(cl, b) + dot(ch, xlt[:, cols]) - csq
                l = l.reshape(rows_n // 8, 8, 256)
                m = jnp.max(l, axis=0)
                e = jnp.exp2(l - m[None])
                e_buf[rows, cols] = e.reshape(rows_n, 256)
                m_buf[first + t, :, cols] = m
                s_buf[first + t, :, cols] = jnp.sum(e, axis=0)
            return 0

        return tile

    lax.fori_loop(0, NX, stage_a(CA, 0, 0), 0)
    lax.fori_loop(0, NTB, stage_a(TB, B0, NX), 0)

    mm = m_buf[...]
    m_loc = jnp.max(jnp.max(mm, axis=0), axis=0, keepdims=True)
    s_loc = jnp.sum(
        jnp.sum(s_buf[...] * jnp.exp2(mm - m_loc[None]), axis=0), axis=0, keepdims=True
    )
    stat[cent] = m_loc + jnp.log(s_loc) * LOG2E
    pl.semaphore_wait(barrier, (NX - 1) + (NZ - 1) + (NC - 1))
    for d in range(1, NC):
        send(stat.at[cent], stat.at[cent], S_STAT, STAT, at_c(d))
    got(stat.at[pl.ds(0, NC - 1)], STAT)
    parts = stat[...]
    top = jnp.max(parts, axis=0)
    total = jnp.log(jnp.sum(jnp.exp2(parts - top[None]), axis=0))
    lse_out[...] = (top * LN2 + total).reshape(N)
    lse2 = top + total * LOG2E
    f_buf[...] = jnp.exp2(mm - lse2[None])

    def block_b(pieces, f):
        hs, ls = [], []
        for rows in pieces:
            n = rows.size
            p = (e_buf[rows, :].reshape(n // 8, 8, N) * f[None]).reshape(n, N)
            w = p[:, 0:128]
            for q in range(1, N // 128):
                w = w + p[:, q * 128 : (q + 1) * 128]
            w8[rows, :] = w
            hi, lo = split(p)
            hs.append(hi)
            ls.append(lo)
        hi = jnp.concatenate(hs, axis=0)
        lo = jnp.concatenate(ls, axis=0)
        r = dot(hi, xh[...]) + dot(lo, xh[...]) + dot(hi, xl[...])
        at = 0
        for rows in pieces:
            numer[rows, :] = r[at : at + rows.size]
            at += rows.size

    def rows_a(dx, dz, off=0, n=RA):
        return pl.ds(pl.multiple_of(mod(x + dx, NX) * CA + mod(z + dz, NZ) * RA + off, 8), n)

    def rows_b(dz, dx, off=0, n=RB):
        return pl.ds(pl.multiple_of(B0 + mod(z + dz, NZ) * CB + mod(x + dx, NX) * RB + off, 8), n)

    def chunk_rows_b(dz, off=0, n=CB):
        return pl.ds(pl.multiple_of(B0 + mod(z + dz, NZ) * CB + off, 8), n)

    def add(rows, ref):
        numer[rows, :] += ref[...]

    HA, HB = RA // 2, RB // 2
    CQ = CB // Q
    HQ = CQ // 2

    SIDES = ((0, 1), (1, -1))

    def a1_send(i):
        for e, sg in SIDES:
            send(numer.at[rows_a(2, ORDER_RS[i], e * HA, HA)], ra1.at[i, e], S_A1, A1 + i, at_x(sg))

    def a1_step(i):
        o = ORDER_RS[i]
        got(ra1.at[i], A1 + i)
        for e, sg in SIDES:
            add(rows_a(sg, o, e * HA, HA), ra1.at[i, e])
            send(numer.at[rows_a(sg, o)], ra2.at[i, e], S_A2, A2 + i, at_x(sg))

    def a2_step(i):
        got(ra2.at[i], A2 + i)
        numer[rows_a(0, ORDER_RS[i]), :] += ra2[i, 0] + ra2[i, 1]

    def az_send0():
        for e, sg in SIDES:
            send(numer.at[rows_a(0, 4, e * HA, HA)], raz0.at[e], S_AZ, AZ, at_z(sg))

    def az_step(k):
        got(raz0 if k == 1 else raz.at[k - 2], AZ + k - 1)
        for e, sg in SIDES:
            if k == 1:
                add(rows_a(0, 3 * sg, e * HA, HA), raz0.at[e])
            else:
                add(rows_a(0, (4 - k) * sg), raz.at[k - 2, e])
            send(numer.at[rows_a(0, (4 - k) * sg)], raz.at[k - 1, e], S_AZ, AZ + k, at_z(sg))

    def bz_send0(q):
        for e, sg in SIDES:
            send(
                numer.at[chunk_rows_b(4, q * CQ + e * HQ, HQ)], rbz0.at[q, e],
                S_BZ, BZ + 4 * q, at_z(sg))

    def bz_step(k, q):
        got(rbz0.at[q] if k == 1 else rbz.at[k - 2, q], BZ + 4 * q + k - 1)
        for e, sg in SIDES:
            if k == 1:
                add(chunk_rows_b(3 * sg, q * CQ + e * HQ, HQ), rbz0.at[q, e])
            else:
                add(chunk_rows_b((4 - k) * sg, q * CQ, CQ), rbz.at[k - 2, q, e])
            send(
                numer.at[chunk_rows_b((4 - k) * sg, q * CQ, CQ)], rbz.at[k - 1, q, e],
                S_BZ, BZ + 4 * q + k, at_z(sg))

    def bz_last(q):
        got(rbz.at[2, q], BZ + 4 * q + 3)
        numer[chunk_rows_b(0, q * CQ, CQ), :] += rbz[2, q, 0] + rbz[2, q, 1]

    def owner_weights(i, _):
        xd, zd = i // NZ, lax.rem(i, NZ)
        a = w8[pl.ds(pl.multiple_of(xd * CA + zd * RA, 8), RA), :]
        b = w8[pl.ds(pl.multiple_of(B0 + zd * CB + xd * RB, 8), RB), :]
        t = jnp.concatenate([a, b], axis=0).T
        wown[xd, pl.ds(zd, 1), :] = jnp.sum(t, axis=0, keepdims=True)
        return 0

    def weights(k):
        lax.fori_loop(8 * k, 8 * k + 8, owner_weights, 0)

    def weights_x():
        for d in range(1, NX):
            send(wown.at[mod(x + d, NX)], rw1.at[d - 1], S_W1, W1, at_x(d))

    def weights_z():
        got(rw1, W1)
        w = wown[x] + rw1[0] + rw1[1] + rw1[2]
        for s in range(NZ):
            w2s[s] = w[s : s + 1, :]
        for d in range(1, NZ):
            send(w2s.at[mod(z + d, NZ)], rw2.at[d - 1], S_W2, W2, at_z(d))

    def weights_own():
        got(rw2, W2)
        w = w2s[z]
        for d in range(1, NZ):
            w = w + rw2[d - 1]
        den[...] = jnp.broadcast_to(w, (RA + RB, RA + RB)).T + PRIOR

    def bx_send():
        for d in range(1, NX):
            send(numer.at[rows_b(0, d)], rbx.at[d - 1], S_BX, BX, at_x(d))

    def finish(mine, rows, total_rows):
        q = den[mine, :]
        q = jnp.concatenate([q, q], axis=1)
        out[rows, :] = (total_rows * (1.0 / XSCALE) + PRIOR * cbuf[rows, :]) / q

    def finish_b():
        got(rbx, BX)
        rows = rows_b(0, 0)
        finish(pl.ds(RA, RB), rows, numer[rows, :] + rbx[0] + rbx[1] + rbx[2])

    def finish_a():
        got(raz.at[2], AZ + 3)
        rows = rows_a(0, 0)
        finish(pl.ds(0, RA), rows, numer[rows, :] + raz[2, 0] + raz[2, 1])

    def give(rows, kind, k, dev):
        send(out.at[rows], out.at[rows], kind, k, dev)

    def gaz_send(k):
        for e, sg in SIDES:
            if k < 3:
                give(rows_a(0, -k * sg), S_GAZ, GAZ + k, at_z(sg))
            else:
                give(rows_a(0, -3 * sg, e * HA, HA), S_GAZ, GAZ + k, at_z(sg))

    def gaz_got(k):
        got(numer.at[pl.ds(0, 2 * RA if k < 3 else RA)], GAZ + k)

    def ga1_send(i):
        for _, sg in SIDES:
            give(rows_a(0, ORDER_AG[i]), S_GA1, GA1 + i, at_x(sg))

    def ga2_send(i):
        give(rows_a(0, ORDER_AG[i]), S_GA2, GA2 + i, at_x(2))

    def ga2_step(i):
        got(numer.at[pl.ds(0, 2 * RA)], GA1 + i)
        for e, sg in SIDES:
            give(rows_a(-sg, ORDER_AG[i], e * HA, HA), S_GA2, GA2 + i, at_x(sg))

    def ga2_got(i):
        got(numer.at[pl.ds(0, RA)], GA2 + i)

    def ga2_last():
        got(numer.at[pl.ds(0, 2 * RA)], GA1 + 7)
        ga2_got(7)

    def gbx_send():
        for d in (2, 1, 3):
            give(rows_b(0, 0), S_GBX, GBX, at_x(d))

    def gbz_send(k, j):
        t = ORDER_T[j]
        for e, sg in SIDES:
            if k < 3:
                give(rows_b(-k * sg, t), S_GBZ, GBZ + 4 * j + k, at_z(sg))
            else:
                give(rows_b(-3 * sg, t, e * HB, HB), S_GBZ, GBZ + 4 * j + k, at_z(sg))

    def gbz_first():
        got(numer.at[pl.ds(0, 3 * RB)], GBX)
        for j in (1, 2, 3):
            gbz_send(0, j)

    def gbz_got(k, j):
        got(numer.at[pl.ds(0, 2 * RB if k < 3 else RB)], GBZ + 4 * j + k)

    def gbz_step(k, j):
        gbz_got(k, j)
        gbz_send(k + 1, j)

    def blocks(j, _):
        late = j // 6
        r = lax.rem(j, 3)
        dx = (2 - r - r // 2) * (1 - late)
        h = (j // 3) * (1 - late) + (j - 6) * late
        pieces = [rows_a(dx, 4 - 6 * h), rows_a(dx, 3 - 2 * h), rows_a(dx, 2 * h - 3), rows_a(dx, 2 - 2 * h)]
        block_b(pieces, f_buf[mod(x + dx, NX)])

        @pl.when(j == 0)
        def _():
            a1_send(0)

        @pl.when(j == 1)
        def _():
            bz_send0(1)
            a1_send(2)
            a1_send(1)
            bz_send0(0)
            a1_send(3)

        @pl.when(j == 3)
        def _():
            a1_step(0)

        @pl.when(j == 4)
        def _():
            bz_step(1, 1)

        @pl.when(j == 5)
        def _():
            a1_send(4)
            a1_send(6)

        @pl.when(j == 6)
        def _():
            a1_send(5)
            a2_step(0)
            az_send0()
            a1_step(3)
            a1_send(7)
            bz_step(1, 0)

        @pl.when(j == 7)
        def _():
            a2_step(1)
            bz_step(2, 1)

        dz = 4 + (1 - 2 * lax.rem(j, 2)) * ((j + 1) // 2)
        block_b([chunk_rows_b(dz)], f_buf[NX + mod(z + dz, NZ) // (NZ // NTB)])

        @pl.when(j == 4)
        def _():
            a1_step(1)
            a1_step(2)

        return 0

    lax.fori_loop(0, 8, blocks, 0)

    weights(0)
    a2_step(2)
    az_step(1)
    weights(1)
    a1_step(4)
    weights(2)
    bz_step(2, 0)
    a1_step(5)
    a1_step(6)
    weights(3)
    weights_x()
    bz_step(3, 1)
    a2_step(3)
    a1_step(7)
    a2_step(4)
    az_step(2)
    bz_step(3, 0)
    a2_step(5)
    bz_last(1)
    a2_step(6)
    weights_z()
    az_step(3)
    a2_step(7)
    bz_last(0)
    bx_send()
    weights_own()
    finish_a()
    gaz_send(0)
    ga1_send(0)
    finish_b()
    gbx_send()
    gbz_send(0, 0)
    gaz_got(0)
    gaz_send(1)
    ga1_send(1)
    ga1_send(2)
    ga2_step(0)
    gbz_step(0, 0)
    gbz_first()
    gaz_got(1)
    gaz_send(2)
    ga1_send(3)
    ga2_step(1)
    ga1_send(4)
    gbz_step(1, 0)
    ga2_step(2)
    gbz_step(0, 1)
    ga2_got(0)
    gbz_step(0, 3)
    gbz_step(0, 2)
    ga2_step(3)
    ga2_got(1)
    gaz_got(2)
    gaz_send(3)
    ga1_send(6)
    ga1_send(5)
    ga2_step(4)
    gbz_step(2, 0)
    ga2_got(2)
    gbz_step(1, 1)
    ga2_got(3)
    gbz_step(1, 3)
    gbz_step(1, 2)
    ga2_step(6)
    gaz_got(3)
    ga1_send(7)
    ga2_send(7)
    gbz_got(3, 0)
    ga2_step(5)
    gbz_step(2, 1)
    ga2_got(4)
    gbz_step(2, 3)
    ga2_got(6)
    gbz_step(2, 2)
    gbz_got(3, 1)
    gbz_got(3, 3)
    ga2_last()
    gbz_got(3, 2)
    ga2_got(5)
    sent(stat.at[pl.ds(0, NC - 1)], S_STAT)
    sent(rw1, S_W1)
    sent(rw2, S_W2)
    sent(rbx, S_BX)
    sent(rbx, S_GBX)
    sent(ra1, S_A1)
    sent(ra2, S_A2)
    for kind, rows in (
        (S_AZ, 2 * (3 * RA + HA)), (S_GAZ, 2 * (3 * RA + HA)), (S_GA1, 16 * RA), (S_GA2, 8 * RA),
        (S_BZ, 2 * (3 * CB + CB // 2)), (S_GBZ, 2 * (3 * CB + CB // 2)),
    ):
        sent(numer.at[pl.ds(0, rows)], kind)


def local(vectors, centroids):
    f32, bf16 = jnp.float32, jnp.bfloat16
    V = pltpu.VMEM
    refined, lse = pl.pallas_call(
        kernel,
        out_shape=(
            V((KP, D), f32),
            V((N,), f32),
        ),
        in_specs=[pl.BlockSpec(memory_space=pl.ANY)] * 2,
        out_specs=[pl.BlockSpec(memory_space=pltpu.VMEM)] * 2,
        scratch_shapes=[
            V((N, D), f32), V((KP, D), f32),
            V((N, D), bf16), V((N, D), bf16), V((D, N), bf16), V((D, N), bf16),
            V((KP, N), f32), V((NT, 8, N), f32), V((NT, 8, N), f32), V((NT, 8, N), f32),
            V((NC, 1, N), f32), V((KP, D), f32), V((KP, 128), f32),
            V((NX, NZ, 128), f32), V((NX - 1, NZ, 128), f32),
            V((NZ, 1, 128), f32), V((NZ - 1, 1, 128), f32),
            V((8, 2, RA // 2, D), f32), V((8, 2, RA, D), f32),
            V((2, RA // 2, D), f32), V((3, 2, RA, D), f32),
            V((Q, 2, CB // Q // 2, D), f32), V((3, Q, 2, CB // Q, D), f32),
            V((NX - 1, RB, D), f32),
            V((RA + RB, RA + RB), f32),
            pltpu.SemaphoreType.DMA((NSEND,)), pltpu.SemaphoreType.DMA((NRECV,)),
            pltpu.SemaphoreType.DMA((NT + 4,)),
        ],
        compiler_params=pltpu.CompilerParams(
            collective_id=0, has_side_effects=True, vmem_limit_bytes=50 * 1024 * 1024
        ),
    )(vectors, centroids)
    return refined, lse


def solution(mesh):
    return jax.shard_map(
        local,
        mesh=mesh,
        in_specs=(P("item", None), P("cent", None)),
        out_specs=(P("cent", None), P("item")),
        check_vma=False,
    )
```

profile of v0, /device:TPU:2, one launch (start us, length us, event | category | flops | bytes accessed | tf_op | source)
XLA Modules:
  0.0 85.2 jit_solution(10521738839639062281)
XLA Ops:
  0.6 81.9 %shard_map.41 = (f32[4096,256]{1,0:T(8,128)S(1)}, f32[1024]{0:T(1024)S(1)}) custom-call(f32[1024,256]{1,0:T(8,128)} %x_hbm.1, f32[4096,256]{1,0:T(8,128)} %c_hbm.1), custom_call_target="tpu_custom_call" | custom-call | tf_op jit(solution)/shard_map/pallas_call | solution.py:521
  82.6 2.0 %copy.6 = f32[4096,256]{1,0:T(8,128)} copy(f32[4096,256]{1,0:T(8,128)S(1)} %get-tuple-element.2) | data formatting | bytes 8388608
  84.6 0.6 copy.7
where the time goes:
time: 85.2 us
  Pallas kernels  81.9 us (96%)
  local copies, waits for them, and re-layouts  2.61 us (3%)
    pallas_call x1, Pallas kernels, local(): pl.pallas_call(kernel, out_shape=(V((KP, D), f32), V((N,), f32)), in_spec...  81.9 us
    unnamed x2, local copies, waits for them, and re-layouts  2.61 us

commit v1 on v0

--- a/solution.py
+++ b/solution.py
@@ -258,16 +258,15 @@
         got(rbz.at[2, q], BZ + 4 * q + 3)
         numer[chunk_rows_b(0, q * CQ, CQ), :] += rbz[2, q, 0] + rbz[2, q, 1]
 
-    def owner_weights(i, _):
-        xd, zd = i // NZ, lax.rem(i, NZ)
-        a = w8[pl.ds(pl.multiple_of(xd * CA + zd * RA, 8), RA), :]
-        b = w8[pl.ds(pl.multiple_of(B0 + zd * CB + xd * RB, 8), RB), :]
+    def owner_weights(xd, zd):
+        a = w8[pl.ds(xd * CA + zd * RA, RA), :]
+        b = w8[pl.ds(B0 + zd * CB + xd * RB, RB), :]
         t = jnp.concatenate([a, b], axis=0).T
-        wown[xd, pl.ds(zd, 1), :] = jnp.sum(t, axis=0, keepdims=True)
-        return 0
+        wown[xd, zd : zd + 1, :] = jnp.sum(t, axis=0, keepdims=True)
 
     def weights(k):
-        lax.fori_loop(8 * k, 8 * k + 8, owner_weights, 0)
+        for i in range(8 * k, 8 * k + 8):
+            owner_weights(*divmod(i, NZ))
 
     def weights_x():
         for d in range(1, NX):
@@ -363,91 +362,75 @@
         gbz_got(k, j)
         gbz_send(k + 1, j)
 
-    def blocks(j, _):
-        late = j // 6
-        r = lax.rem(j, 3)
-        dx = (2 - r - r // 2) * (1 - late)
-        h = (j // 3) * (1 - late) + (j - 6) * late
-        pieces = [rows_a(dx, 4 - 6 * h), rows_a(dx, 3 - 2 * h), rows_a(dx, 2 * h - 3), rows_a(dx, 2 - 2 * h)]
-        block_b(pieces, f_buf[mod(x + dx, NX)])
-
-        @pl.when(j == 0)
-        def _():
-            a1_send(0)
-
-        @pl.when(j == 1)
-        def _():
-            bz_send0(1)
-            a1_send(2)
-            a1_send(1)
-            bz_send0(0)
-            a1_send(3)
-
-        @pl.when(j == 3)
-        def _():
-            a1_step(0)
-
-        @pl.when(j == 4)
-        def _():
-            bz_step(1, 1)
-
-        @pl.when(j == 5)
-        def _():
-            a1_send(4)
-            a1_send(6)
-
-        @pl.when(j == 6)
-        def _():
-            a1_send(5)
-            a2_step(0)
-            az_send0()
-            a1_step(3)
-            a1_send(7)
-            bz_step(1, 0)
-
-        @pl.when(j == 7)
-        def _():
-            a2_step(1)
-            bz_step(2, 1)
-
-        dz = 4 + (1 - 2 * lax.rem(j, 2)) * ((j + 1) // 2)
+    def part_a(dx, half):
+        order = ORDER_RS[4 * half : 4 * half + 4]
+        block_b([rows_a(dx, o) for o in order], f_buf[mod(x + dx, NX)])
+
+    def part_b(dz):
         block_b([chunk_rows_b(dz)], f_buf[NX + mod(z + dz, NZ) // (NZ // NTB)])
 
-        @pl.when(j == 4)
-        def _():
-            a1_step(1)
-            a1_step(2)
-
-        return 0
-
-    lax.fori_loop(0, 8, blocks, 0)
-
+    part_a(2, 0)
+    a1_send(0)
+    part_b(4)
+    bz_send0(1)
+    a1_send(2)
+    a1_send(1)
+    part_a(2, 1)
+    a1_send(4)
+    part_a(1, 0)
+    part_a(0, 0)
+    part_a(-1, 0)
+    part_b(-2)
+    a1_step(0)
+    part_b(1)
+    part_b(-3)
+    a1_step(2)
+    bz_send0(0)
+    part_b(3)
+    bz_step(1, 1)
+    a1_step(1)
+    part_a(1, 1)
+    part_b(-1)
+    a1_send(3)
+    part_a(-1, 1)
+    a1_step(4)
+    a1_send(5)
+    part_a(0, 1)
+    a2_step(0)
+    az_send0()
+    part_b(0)
+    bz_step(1, 0)
+    a1_send(6)
+    part_b(2)
+    a1_send(7)
     weights(0)
+    weights(1)
+    bz_step(2, 1)
+    weights(2)
     a2_step(2)
+    weights(3)
+    weights_x()
+    a2_step(1)
     az_step(1)
-    weights(1)
-    a1_step(4)
-    weights(2)
+    a1_step(3)
     bz_step(2, 0)
+    a2_step(4)
     a1_step(5)
     a1_step(6)
-    weights(3)
-    weights_x()
     bz_step(3, 1)
+    a1_step(7)
+    weights_z()
     a2_step(3)
-    a1_step(7)
-    a2_step(4)
     az_step(2)
     bz_step(3, 0)
     a2_step(5)
     bz_last(1)
+    weights_own()
     a2_step(6)
-    weights_z()
     az_step(3)
     a2_step(7)
     bz_last(0)
     bx_send()
-    weights_own()
     finish_a()
     gaz_send(0)
     ga1_send(0)
@@ -456,51 +439,52 @@
     gbz_send(0, 0)
     gaz_got(0)
     gaz_send(1)
+    ga2_step(0)
+    ga1_send(2)
     ga1_send(1)
-    ga1_send(2)
-    ga2_step(0)
     gbz_step(0, 0)
     gbz_first()
+    ga2_got(0)
     gaz_got(1)
     gaz_send(2)
+    ga1_send(4)
     ga1_send(3)
+    ga2_step(2)
+    gbz_step(1, 0)
+    gbz_step(0, 2)
     ga2_step(1)
-    ga1_send(4)
-    gbz_step(1, 0)
-    ga2_step(2)
     gbz_step(0, 1)
-    ga2_got(0)
     gbz_step(0, 3)
-    gbz_step(0, 2)
-    ga2_step(3)
-    ga2_got(1)
+    ga2_step(4)
     gaz_got(2)
     gaz_send(3)
+    ga1_send(5)
     ga1_send(6)
-    ga1_send(5)
-    ga2_step(4)
+    ga2_step(3)
+    ga2_got(2)
     gbz_step(2, 0)
-    ga2_got(2)
+    ga2_got(1)
+    gbz_step(1, 2)
+    ga2_got(4)
     gbz_step(1, 1)
-    ga2_got(3)
     gbz_step(1, 3)
-    gbz_step(1, 2)
-    ga2_step(6)
+    ga2_step(5)
     gaz_got(3)
     ga1_send(7)
     ga2_send(7)
     gbz_got(3, 0)
-    ga2_step(5)
+    ga2_step(6)
+    gbz_step(2, 2)
+    ga2_got(3)
     gbz_step(2, 1)
-    ga2_got(4)
+    ga2_got(5)
     gbz_step(2, 3)
+    gbz_got(3, 2)
+    gbz_got(3, 1)
+    ga2_last()
+    gbz_got(3, 3)
     ga2_got(6)
-    gbz_step(2, 2)
-    gbz_got(3, 1)
-    gbz_got(3, 3)
-    ga2_last()
-    gbz_got(3, 2)
-    ga2_got(5)
+
     sent(stat.at[pl.ds(0, NC - 1)], S_STAT)
     sent(rw1, S_W1)
     sent(rw2, S_W2)

time: 85.2 us -> 83.8 us (0.984)
  Pallas kernels: 81.9 us -> 80.4 us
    pallas_call x1, Pallas kernels: 81.9 us -> 80.4 us  [local(): pl.pallas_call(kernel, out_shape=(V((KP, D), f32), V((N,), f32)), in_spec...]
where the time goes in v1:
time: 83.8 us; the launch traced here: 83.6 us
  Pallas kernels  80.4 us (96%)
  local copies, waits for them, and re-layouts  2.61 us (3%)
    pallas_call x1, Pallas kernels, local(): pl.pallas_call(kernel, out_shape=(V((KP, D), f32), V((N,), f32)), in_spec...  80.4 us
    unnamed x2, local copies, waits for them, and re-layouts  2.61 us

profile of v1, /device:TPU:2, one launch (start us, length us, event | category | flops | bytes accessed | tf_op | source)
XLA Modules:
  0.0 83.6 jit_solution(2033184880135843998)
XLA Ops:
  0.6 80.4 %shard_map.41 = (f32[4096,256]{1,0:T(8,128)S(1)}, f32[1024]{0:T(1024)S(1)}) custom-call(f32[1024,256]{1,0:T(8,128)} %x_hbm.1, f32[4096,256]{1,0:T(8,128)} %c_hbm.1), custom_call_target="tpu_custom_call" | custom-call | tf_op jit(solution)/shard_map/pallas_call | solution.py:505
  81.0 2.0 %copy.6 = f32[4096,256]{1,0:T(8,128)} copy(f32[4096,256]{1,0:T(8,128)S(1)} %get-tuple-element.2) | data formatting | bytes 8388608
  83.0 0.6 copy.7

commit v2 on v1

--- a/solution.py
+++ b/solution.py
@@ -26,17 +26,24 @@
 NTB = NZ * CB // TB
 NT = NX + NTB
 Q = 2
-
-STAT, W1, W2, BX, GBX = range(5)
-A1 = 5
-A2 = A1 + 8
-AZ = A2 + 8
-BZ = AZ + 4
+PA, PB = RA // Q, RB // Q
+CQ = NX * PB
+HALF_A = (((0, 24), (24, 16)), ((0, 16), (16, 24)))
+HALF_B = (((0, 16), (16, 8)), ((0, 8), (8, 16)))
+
+STAT, W1, W2 = range(3)
+BX = 3
+GBX = BX + Q
+A1 = GBX + Q
+A2 = A1 + 8 * Q
+AZ = A2 + 8 * Q
+BZ = AZ + 4 * Q
 GAZ = BZ + 4 * Q
-GA1 = GAZ + 4
-GA2 = GA1 + 8
-GBZ = GA2 + 8
-NRECV = GBZ + 16
+GA1 = GAZ + 4 * Q
+GA2 = GA1 + 8 * Q
+GBZ = GA2 + Q
+GBL = GBZ + 12 * Q
+NRECV = GBL + Q
 S_STAT, S_W1, S_W2, S_BX, S_GBX, S_A1, S_A2, S_AZ, S_BZ, S_GAZ, S_GA1, S_GA2, S_GBZ = range(13)
 NSEND = 13
 
@@ -167,8 +174,8 @@
     parts = stat[...]
     top = jnp.max(parts, axis=0)
     total = jnp.log(jnp.sum(jnp.exp2(parts - top[None]), axis=0))
-    lse_out[...] = (top * LN2 + total).reshape(N)
     lse2 = top + total * LOG2E
+    lse_out[...] = lse2.reshape(N)
     f_buf[...] = jnp.exp2(mm - lse2[None])
 
     def block_b(pieces, f):
@@ -191,11 +198,13 @@
             numer[rows, :] = r[at : at + rows.size]
             at += rows.size
 
-    def rows_a(dx, dz, off=0, n=RA):
-        return pl.ds(pl.multiple_of(mod(x + dx, NX) * CA + mod(z + dz, NZ) * RA + off, 8), n)
-
-    def rows_b(dz, dx, off=0, n=RB):
-        return pl.ds(pl.multiple_of(B0 + mod(z + dz, NZ) * CB + mod(x + dx, NX) * RB + off, 8), n)
+    def rows_a(dx, dz, l, off=0, n=PA):
+        start = mod(x + dx, NX) * CA + l * NZ * PA + mod(z + dz, NZ) * PA + off
+        return pl.ds(pl.multiple_of(start, 8), n)
+
+    def rows_b(dz, dx, l, off=0, n=PB):
+        start = B0 + mod(z + dz, NZ) * CB + l * CQ + mod(x + dx, NX) * PB + off
+        return pl.ds(pl.multiple_of(start, 8), n)
 
     def chunk_rows_b(dz, off=0, n=CB):
         return pl.ds(pl.multiple_of(B0 + mod(z + dz, NZ) * CB + off, 8), n)
@@ -203,39 +212,46 @@
     def add(rows, ref):
         numer[rows, :] += ref[...]
 
-    HA, HB = RA // 2, RB // 2
-    CQ = CB // Q
     HQ = CQ // 2
-
     SIDES = ((0, 1), (1, -1))
 
-    def a1_send(i):
-        for e, sg in SIDES:
-            send(numer.at[rows_a(2, ORDER_RS[i], e * HA, HA)], ra1.at[i, e], S_A1, A1 + i, at_x(sg))
-
-    def a1_step(i):
+    def a1_send(l, i):
+        for e, sg in SIDES:
+            off, n = HALF_A[l][e]
+            send(
+                numer.at[rows_a(2, ORDER_RS[i], l, off, n)], ra1.at[l, i, pl.ds(off, n)],
+                S_A1, A1 + 8 * l + i, at_x(sg))
+
+    def a1_step(l, i):
         o = ORDER_RS[i]
-        got(ra1.at[i], A1 + i)
-        for e, sg in SIDES:
-            add(rows_a(sg, o, e * HA, HA), ra1.at[i, e])
-            send(numer.at[rows_a(sg, o)], ra2.at[i, e], S_A2, A2 + i, at_x(sg))
-
-    def a2_step(i):
-        got(ra2.at[i], A2 + i)
-        numer[rows_a(0, ORDER_RS[i]), :] += ra2[i, 0] + ra2[i, 1]
-
-    def az_send0():
-        for e, sg in SIDES:
-            send(numer.at[rows_a(0, 4, e * HA, HA)], raz0.at[e], S_AZ, AZ, at_z(sg))
-
-    def az_step(k):
-        got(raz0 if k == 1 else raz.at[k - 2], AZ + k - 1)
+        got(ra1.at[l, i], A1 + 8 * l + i)
+        for e, sg in SIDES:
+            off, n = HALF_A[l][e]
+            add(rows_a(sg, o, l, off, n), ra1.at[l, i, pl.ds(off, n)])
+            send(numer.at[rows_a(sg, o, l)], ra2.at[l, i, e], S_A2, A2 + 8 * l + i, at_x(sg))
+
+    def a2_step(l, i):
+        got(ra2.at[l, i], A2 + 8 * l + i)
+        numer[rows_a(0, ORDER_RS[i], l), :] += ra2[l, i, 0] + ra2[l, i, 1]
+
+    def az_send0(l):
+        for e, sg in SIDES:
+            off, n = HALF_A[l][e]
+            send(
+                numer.at[rows_a(0, 4, l, off, n)], raz0.at[l, pl.ds(off, n)],
+                S_AZ, AZ + 4 * l, at_z(sg))
+
+    def az_step(l, k):
+        got(raz0.at[l] if k == 1 else raz.at[l, k - 2], AZ + 4 * l + k - 1)
         for e, sg in SIDES:
             if k == 1:
-                add(rows_a(0, 3 * sg, e * HA, HA), raz0.at[e])
+                off, n = HALF_A[l][e]
+                add(rows_a(0, 3 * sg, l, off, n), raz0.at[l, pl.ds(off, n)])
             else:
-                add(rows_a(0, (4 - k) * sg), raz.at[k - 2, e])
-            send(numer.at[rows_a(0, (4 - k) * sg)], raz.at[k - 1, e], S_AZ, AZ + k, at_z(sg))
+                add(rows_a(0, (4 - k) * sg, l), raz.at[l, k - 2, e])
+            send(
+                numer.at[rows_a(0, (4 - k) * sg, l)], raz.at[l, k - 1, e],
+                S_AZ, AZ + 4 * l + k, at_z(sg))
 
     def bz_send0(q):
         for e, sg in SIDES:
@@ -259,9 +275,9 @@
         numer[chunk_rows_b(0, q * CQ, CQ), :] += rbz[2, q, 0] + rbz[2, q, 1]
 
     def owner_weights(xd, zd):
-        a = w8[pl.ds(xd * CA + zd * RA, RA), :]
-        b = w8[pl.ds(B0 + zd * CB + xd * RB, RB), :]
-        t = jnp.concatenate([a, b], axis=0).T
+        a, b = xd * CA + zd * PA, B0 + zd * CB + xd * PB
+        rows = [pl.ds(a + l * NZ * PA, PA) for l in range(Q)] + [pl.ds(b + l * CQ, PB) for l in range(Q)]
+        t = jnp.concatenate([w8[r, :] for r in rows], axis=0).T
         wown[xd, zd : zd + 1, :] = jnp.sum(t, axis=0, keepdims=True)
 
     def weights(k):
@@ -287,203 +303,256 @@
             w = w + rw2[d - 1]
         den[...] = jnp.broadcast_to(w, (RA + RB, RA + RB)).T + PRIOR
 
-    def bx_send():
+    def bx_send(l):
         for d in range(1, NX):
-            send(numer.at[rows_b(0, d)], rbx.at[d - 1], S_BX, BX, at_x(d))
+            send(numer.at[rows_b(0, d, l)], rbx.at[l, d - 1], S_BX, BX + l, at_x(d))
 
     def finish(mine, rows, total_rows):
         q = den[mine, :]
         q = jnp.concatenate([q, q], axis=1)
         out[rows, :] = (total_rows * (1.0 / XSCALE) + PRIOR * cbuf[rows, :]) / q
 
-    def finish_b():
-        got(rbx, BX)
-        rows = rows_b(0, 0)
-        finish(pl.ds(RA, RB), rows, numer[rows, :] + rbx[0] + rbx[1] + rbx[2])
-
-    def finish_a():
-        got(raz.at[2], AZ + 3)
-        rows = rows_a(0, 0)
-        finish(pl.ds(0, RA), rows, numer[rows, :] + raz[2, 0] + raz[2, 1])
+    def finish_b(l):
+        got(rbx.at[l], BX + l)
+        rows = rows_b(0, 0, l)
+        finish(pl.ds(RA + l * PB, PB), rows, numer[rows, :] + rbx[l, 0] + rbx[l, 1] + rbx[l, 2])
+
+    def finish_a(l):
+        got(raz.at[l, 2], AZ + 4 * l + 3)
+        rows = rows_a(0, 0, l)
+        finish(pl.ds(l * PA, PA), rows, numer[rows, :] + raz[l, 2, 0] + raz[l, 2, 1])
 
     def give(rows, kind, k, dev):
         send(out.at[rows], out.at[rows], kind, k, dev)
 
-    def gaz_send(k):
+    def gaz_send(l, k):
+        for e, sg in SIDES:
+            rows = rows_a(0, -k * sg, l) if k < 3 else rows_a(0, -3 * sg, l, *HALF_A[l][e])
+            give(rows, S_GAZ, GAZ + 4 * l + k, at_z(sg))
+
+    def gaz_got(l, k):
+        got(numer.at[pl.ds(0, 2 * PA if k < 3 else PA)], GAZ + 4 * l + k)
+
+    def ga1_send(l, i):
+        for _, sg in SIDES:
+            give(rows_a(0, ORDER_AG[i], l), S_GA1, GA1 + 8 * l + i, at_x(sg))
+
+    def ga1_got(l, i):
+        got(numer.at[pl.ds(0, 2 * PA)], GA1 + 8 * l + i)
+
+    def ga2_send(l, i):
+        give(rows_a(0, ORDER_AG[i], l), S_GA2, GA2 + l, at_x(2))
+
+    def ga2_step(l, i):
+        ga1_got(l, i)
+        for e, sg in SIDES:
+            give(rows_a(-sg, ORDER_AG[i], l, *HALF_A[l][e]), S_GA2, GA2 + l, at_x(sg))
+
+    def gbx_send(l):
+        for d in (2, 1, 3):
+            give(rows_b(0, 0, l), S_GBX, GBX + l, at_x(d))
+
+    def gbz_send(l, k, j):
+        t = ORDER_T[j]
         for e, sg in SIDES:
             if k < 3:
-                give(rows_a(0, -k * sg), S_GAZ, GAZ + k, at_z(sg))
+                give(rows_b(-k * sg, t, l), S_GBZ, GBZ + 12 * l + 3 * j + k, at_z(sg))
             else:
-                give(rows_a(0, -3 * sg, e * HA, HA), S_GAZ, GAZ + k, at_z(sg))
-
-    def gaz_got(k):
-        got(numer.at[pl.ds(0, 2 * RA if k < 3 else RA)], GAZ + k)
-
-    def ga1_send(i):
-        for _, sg in SIDES:
-            give(rows_a(0, ORDER_AG[i]), S_GA1, GA1 + i, at_x(sg))
-
-    def ga2_send(i):
-        give(rows_a(0, ORDER_AG[i]), S_GA2, GA2 + i, at_x(2))
-
-    def ga2_step(i):
-        got(numer.at[pl.ds(0, 2 * RA)], GA1 + i)
-        for e, sg in SIDES:
-            give(rows_a(-sg, ORDER_AG[i], e * HA, HA), S_GA2, GA2 + i, at_x(sg))
-
-    def ga2_got(i):
-        got(numer.at[pl.ds(0, RA)], GA2 + i)
-
-    def ga2_last():
-        got(numer.at[pl.ds(0, 2 * RA)], GA1 + 7)
-        ga2_got(7)
-
-    def gbx_send():
-        for d in (2, 1, 3):
-            give(rows_b(0, 0), S_GBX, GBX, at_x(d))
-
-    def gbz_send(k, j):
-        t = ORDER_T[j]
-        for e, sg in SIDES:
-            if k < 3:
-                give(rows_b(-k * sg, t), S_GBZ, GBZ + 4 * j + k, at_z(sg))
-            else:
-                give(rows_b(-3 * sg, t, e * HB, HB), S_GBZ, GBZ + 4 * j + k, at_z(sg))
-
-    def gbz_first():
-        got(numer.at[pl.ds(0, 3 * RB)], GBX)
+                give(rows_b(-3 * sg, t, l, *HALF_B[l][e]), S_GBZ, GBL + l, at_z(sg))
+
+    def gbz_first(l):
+        got(numer.at[pl.ds(0, 3 * PB)], GBX + l)
         for j in (1, 2, 3):
-            gbz_send(0, j)
-
-    def gbz_got(k, j):
-        got(numer.at[pl.ds(0, 2 * RB if k < 3 else RB)], GBZ + 4 * j + k)
-
-    def gbz_step(k, j):
-        gbz_got(k, j)
-        gbz_send(k + 1, j)
-
-    def part_a(dx, half):
-        order = ORDER_RS[4 * half : 4 * half + 4]
-        block_b([rows_a(dx, o) for o in order], f_buf[mod(x + dx, NX)])
+            gbz_send(l, 0, j)
+
+    def gbz_step(l, k, j):
+        got(numer.at[pl.ds(0, 2 * PB)], GBZ + 12 * l + 3 * j + k)
+        gbz_send(l, k + 1, j)
+
+    def part_a(dx, l):
+        start = mod(x + dx, NX) * CA + l * NZ * PA
+        block_b([pl.ds(pl.multiple_of(start, 8), NZ * PA)], f_buf[mod(x + dx, NX)])
 
     def part_b(dz):
         block_b([chunk_rows_b(dz)], f_buf[NX + mod(z + dz, NZ) // (NZ // NTB)])
 
+    part_b(4)
+    bz_send0(0)
+    bz_send0(1)
     part_a(2, 0)
-    a1_send(0)
-    part_b(4)
-    bz_send0(1)
-    a1_send(2)
-    a1_send(1)
+    a1_send(0, 0)
+    a1_send(0, 1)
     part_a(2, 1)
-    a1_send(4)
+    a1_send(1, 3)
+    a1_send(1, 0)
+    a1_send(1, 1)
+    part_b(3)
+    part_b(-3)
     part_a(1, 0)
+    part_a(-1, 0)
+    a1_send(0, 2)
+    a1_send(1, 2)
+    bz_step(1, 0)
+    a1_step(0, 0)
+    a1_send(0, 4)
+    a1_send(1, 4)
+    part_a(1, 1)
+    bz_step(1, 1)
+    a1_send(0, 3)
+    part_a(-1, 1)
+    a1_step(1, 0)
+    a1_step(1, 1)
+    part_a(0, 1)
+    a1_step(0, 1)
+    a1_step(0, 2)
+    part_b(-2)
+    a1_step(1, 2)
     part_a(0, 0)
-    part_a(-1, 0)
-    part_b(-2)
-    a1_step(0)
+    a1_send(0, 5)
+    a2_step(0, 0)
+    az_send0(0)
+    a1_send(0, 6)
+    part_b(2)
+    bz_step(2, 0)
+    a1_step(0, 4)
+    a1_step(1, 4)
+    a1_send(1, 5)
+    a1_send(1, 6)
+    a1_step(0, 3)
+    a1_send(1, 7)
+    a1_send(0, 7)
+    a1_step(1, 3)
+    part_b(-1)
+    a2_step(1, 0)
+    az_send0(1)
     part_b(1)
-    part_b(-3)
-    a1_step(2)
-    bz_send0(0)
-    part_b(3)
-    bz_step(1, 1)
-    a1_step(1)
-    part_a(1, 1)
-    part_b(-1)
-    a1_send(3)
-    part_a(-1, 1)
-    a1_step(4)
-    a1_send(5)
-    part_a(0, 1)
-    a2_step(0)
-    az_send0()
+    bz_step(2, 1)
     part_b(0)
-    bz_step(1, 0)
-    a1_send(6)
-    part_b(2)
-    a1_send(7)
+    a2_step(1, 1)
     weights(0)
     weights(1)
-    bz_step(2, 1)
     weights(2)
-    a2_step(2)
     weights(3)
+    a2_step(0, 1)
     weights_x()
-    a2_step(1)
-    az_step(1)
-    a1_step(3)
-    bz_step(2, 0)
-    a2_step(4)
-    a1_step(5)
-    a1_step(6)
+    a2_step(0, 2)
+    az_step(0, 1)
+    bz_step(3, 0)
+    a2_step(1, 2)
+    az_step(1, 1)
+    a1_step(0, 5)
+    a1_step(0, 6)
+    a2_step(0, 4)
     bz_step(3, 1)
-    a1_step(7)
+    a2_step(1, 4)
+    a1_step(1, 5)
+    a1_step(1, 6)
+    a2_step(0, 3)
+    az_step(0, 2)
+    a1_step(1, 7)
+    a1_step(0, 7)
+    bz_last(0)
+    bx_send(0)
+    a2_step(1, 3)
+    az_step(1, 2)
     weights_z()
-    a2_step(3)
-    az_step(2)
-    bz_step(3, 0)
-    a2_step(5)
+    a2_step(0, 5)
+    a2_step(0, 6)
     bz_last(1)
+    bx_send(1)
+    a2_step(1, 5)
+    az_step(0, 3)
+    a2_step(1, 6)
+    az_step(1, 3)
     weights_own()
-    a2_step(6)
-    az_step(3)
-    a2_step(7)
-    bz_last(0)
-    bx_send()
-    finish_a()
-    gaz_send(0)
-    ga1_send(0)
-    finish_b()
-    gbx_send()
-    gbz_send(0, 0)
-    gaz_got(0)
-    gaz_send(1)
-    ga2_step(0)
-    ga1_send(2)
-    ga1_send(1)
-    gbz_step(0, 0)
-    gbz_first()
-    ga2_got(0)
-    gaz_got(1)
-    gaz_send(2)
-    ga1_send(4)
-    ga1_send(3)
-    ga2_step(2)
-    gbz_step(1, 0)
-    gbz_step(0, 2)
-    ga2_step(1)
-    gbz_step(0, 1)
-    gbz_step(0, 3)
-    ga2_step(4)
-    gaz_got(2)
-    gaz_send(3)
-    ga1_send(5)
-    ga1_send(6)
-    ga2_step(3)
-    ga2_got(2)
-    gbz_step(2, 0)
-    ga2_got(1)
-    gbz_step(1, 2)
-    ga2_got(4)
-    gbz_step(1, 1)
-    gbz_step(1, 3)
-    ga2_step(5)
-    gaz_got(3)
-    ga1_send(7)
-    ga2_send(7)
-    gbz_got(3, 0)
-    ga2_step(6)
-    gbz_step(2, 2)
-    ga2_got(3)
-    gbz_step(2, 1)
-    ga2_got(5)
-    gbz_step(2, 3)
-    gbz_got(3, 2)
-    gbz_got(3, 1)
-    ga2_last()
-    gbz_got(3, 3)
-    ga2_got(6)
+    a2_step(1, 7)
+    a2_step(0, 7)
+    finish_b(0)
+    gbz_send(0, 0, 0)
+    finish_a(0)
+    gaz_send(0, 0)
+    gbx_send(0)
+    ga1_send(0, 0)
+    finish_b(1)
+    gbx_send(1)
+    finish_a(1)
+    ga1_send(1, 0)
+    gaz_send(1, 0)
+    gbz_send(1, 0, 0)
+    gbz_step(0, 0, 0)
+    gaz_got(0, 0)
+    gaz_send(0, 1)
+    ga1_send(0, 1)
+    gbz_first(0)
+    ga1_send(0, 2)
+    gaz_got(1, 0)
+    gaz_send(1, 1)
+    ga1_send(1, 2)
+    ga1_send(1, 1)
+    ga2_step(0, 0)
+    gbz_step(1, 0, 0)
+    gbz_first(1)
+    gbz_step(0, 1, 0)
+    ga2_step(1, 0)
+    gaz_got(0, 1)
+    gaz_send(0, 2)
+    ga1_send(0, 3)
+    ga2_step(0, 1)
+    ga1_send(0, 4)
+    gbz_step(0, 0, 3)
+    ga2_step(0, 2)
+    gbz_step(0, 0, 2)
+    gbz_step(0, 0, 1)
+    ga2_step(1, 2)
+    gaz_got(1, 1)
+    gaz_send(1, 2)
+    ga1_send(1, 4)
+    ga2_step(1, 1)
+    ga1_send(1, 3)
+    gbz_step(1, 1, 0)
+    gbz_step(1, 0, 3)
+    gbz_step(1, 0, 2)
+    ga2_step(0, 3)
+    gbz_step(1, 0, 1)
+    gbz_step(0, 2, 0)
+    ga2_step(0, 4)
+    gaz_got(0, 2)
+    gaz_send(0, 3)
+    ga1_send(0, 6)
+    ga1_send(0, 5)
+    gbz_step(0, 1, 3)
+    gbz_step(0, 1, 2)
+    gbz_step(0, 1, 1)
+    ga2_step(1, 4)
+    gaz_got(1, 2)
+    gaz_send(1, 3)
+    ga1_send(1, 6)
+    ga1_send(1, 5)
+    ga2_step(1, 3)
+    gbz_step(1, 2, 0)
+    gbz_step(1, 1, 3)
+    gbz_step(1, 1, 2)
+    gbz_step(1, 1, 1)
+    ga2_step(0, 6)
+    gaz_got(0, 3)
+    ga1_send(0, 7)
+    ga2_step(0, 5)
+    gbz_step(0, 2, 3)
+    gbz_step(0, 2, 2)
+    gbz_step(0, 2, 1)
+    ga2_step(1, 6)
+    gaz_got(1, 3)
+    ga1_send(1, 7)
+    ga2_send(1, 7)
+    ga2_step(1, 5)
+    gbz_step(1, 2, 3)
+    gbz_step(1, 2, 2)
+    gbz_step(1, 2, 1)
+    ga2_step(0, 7)
+    for l in range(Q):
+        got(numer.at[pl.ds(0, NX * PB)], GBL + l)
+        got(numer.at[pl.ds(0, 8 * PA)], GA2 + l)
+    ga1_got(1, 7)
 
     sent(stat.at[pl.ds(0, NC - 1)], S_STAT)
     sent(rw1, S_W1)
@@ -493,8 +562,8 @@
     sent(ra1, S_A1)
     sent(ra2, S_A2)
     for kind, rows in (
-        (S_AZ, 2 * (3 * RA + HA)), (S_GAZ, 2 * (3 * RA + HA)), (S_GA1, 16 * RA), (S_GA2, 8 * RA),
-        (S_BZ, 2 * (3 * CB + CB // 2)), (S_GBZ, 2 * (3 * CB + CB // 2)),
+        (S_AZ, 7 * RA), (S_GAZ, 7 * RA), (S_GA1, 16 * RA), (S_GA2, 8 * RA),
+        (S_BZ, 7 * CB), (S_GBZ, 7 * CB),
     ):
         sent(numer.at[pl.ds(0, rows)], kind)
 
@@ -517,10 +586,10 @@
             V((NC, 1, N), f32), V((KP, D), f32), V((KP, 128), f32),
             V((NX, NZ, 128), f32), V((NX - 1, NZ, 128), f32),
             V((NZ, 1, 128), f32), V((NZ - 1, 1, 128), f32),
-            V((8, 2, RA // 2, D), f32), V((8, 2, RA, D), f32),
-            V((2, RA // 2, D), f32), V((3, 2, RA, D), f32),
-            V((Q, 2, CB // Q // 2, D), f32), V((3, Q, 2, CB // Q, D), f32),
-            V((NX - 1, RB, D), f32),
+            V((Q, 8, PA, D), f32), V((Q, 8, 2, PA, D), f32),
+            V((Q, PA, D), f32), V((Q, 3, 2, PA, D), f32),
+            V((Q, 2, CQ // 2, D), f32), V((3, Q, 2, CQ, D), f32),
+            V((Q, NX - 1, PB, D), f32),
             V((RA + RB, RA + RB), f32),
             pltpu.SemaphoreType.DMA((NSEND,)), pltpu.SemaphoreType.DMA((NRECV,)),
             pltpu.SemaphoreType.DMA((NT + 4,)),
@@ -529,7 +598,7 @@
             collective_id=0, has_side_effects=True, vmem_limit_bytes=50 * 1024 * 1024
         ),
     )(vectors, centroids)
-    return refined, lse
+    return refined, lse * LN2
 
 
 def solution(mesh):

time: 83.8 us -> 81.5 us (0.973)
  Pallas kernels: 80.4 us -> 78.1 us
    pallas_call x1, Pallas kernels: 80.4 us -> 78.1 us  [local(): pl.pallas_call(kernel, out_shape=(V((KP, D), f32), V((N,), f32)), in_spec...]
    unnamed x2 -> x1, local copies, waits for them, and re-layouts: 2.61 us -> 2.02 us
where the time goes in v2:
time: 81.5 us; the launch traced here: 81.4 us
  Pallas kernels  78.1 us (96%)
  local copies, waits for them, and re-layouts  2.02 us (2%)
    pallas_call x1, Pallas kernels, local(): pl.pallas_call(kernel, out_shape=(V((KP, D), f32), V((N,), f32)), in_spec...  78.1 us
    unnamed x1, local copies, waits for them, and re-layouts  2.02 us

profile of v2, /device:TPU:2, one launch (start us, length us, event | category | flops | bytes accessed | tf_op | source)
XLA Modules:
  0.0 81.4 jit_solution(5363789923048459463)
XLA Ops:
  0.6 78.1 %shard_map.41 = (f32[4096,256]{1,0:T(8,128)S(1)}, f32[1024]{0:T(1024)S(1)}) custom-call(f32[1024,256]{1,0:T(8,128)} %x_hbm.1, f32[4096,256]{1,0:T(8,128)} %c_hbm.1), custom_call_target="tpu_custom_call" | custom-call | tf_op jit(solution)/shard_map/pallas_call | solution.py:574
  78.8 2.0 %copy.5 = f32[4096,256]{1,0:T(8,128)} copy(f32[4096,256]{1,0:T(8,128)S(1)} %get-tuple-element.6) | data formatting | bytes 8388608
  80.8 0.6 broadcast_multiply_fusion

commit v3 on v2

--- a/solution.py
+++ b/solution.py
@@ -56,6 +56,10 @@
     return jnp.dot(a, b, preferred_element_type=jnp.float32)
 
 
+def dot_t(a, b):
+    return lax.dot_general(a, b, (((1,), (1,)), ((), ())), preferred_element_type=jnp.float32)
+
+
 def split(v):
     hi = v.astype(jnp.bfloat16)
     lo = (v - hi.astype(jnp.float32)).astype(jnp.bfloat16)
@@ -64,7 +68,7 @@
 
 def kernel(
     x_hbm, c_hbm, out, lse_out,
-    xbuf, cbuf, xh, xl, xht, xlt, e_buf, m_buf, s_buf, f_buf, stat, numer, w8,
+    xbuf, cbuf, xh, xl, e_buf, m_buf, s_buf, f_buf, stat, numer, w8,
     wown, rw1, w2s, rw2, ra1, ra2, raz0, raz, rbz0, rbz, rbx, den,
     ss, rs, lsem,
 ):
@@ -133,9 +137,6 @@
         hi, lo = split(v)
         xh[rows, :] = hi
         xl[rows, :] = lo
-        hi, lo = split(v.T)
-        xht[:, rows] = hi
-        xlt[:, rows] = lo
 
     def stage_a(rows_n, base, first):
         def tile(t, _):
@@ -146,8 +147,8 @@
             ch, cl = split(c)
             for j in range(N // 256):
                 cols = pl.ds(j * 256, 256)
-                b = xht[:, cols]
-                l = dot(ch, b) + dot(cl, b) + dot(ch, xlt[:, cols]) - csq
+                b = xh[cols, :]
+                l = dot_t(ch, b) + dot_t(cl, b) + dot_t(ch, xl[cols, :]) - csq
                 l = l.reshape(rows_n // 8, 8, 256)
                 m = jnp.max(l, axis=0)
                 e = jnp.exp2(l - m[None])
@@ -168,7 +169,7 @@
     )
     stat[cent] = m_loc + jnp.log(s_loc) * LOG2E
     pl.semaphore_wait(barrier, (NX - 1) + (NZ - 1) + (NC - 1))
-    for d in range(1, NC):
+    for d in (4, 3, 5, 2, 6, 1, 7):
         send(stat.at[cent], stat.at[cent], S_STAT, STAT, at_c(d))
     got(stat.at[pl.ds(0, NC - 1)], STAT)
     parts = stat[...]
@@ -581,7 +582,7 @@
         out_specs=[pl.BlockSpec(memory_space=pltpu.VMEM)] * 2,
         scratch_shapes=[
             V((N, D), f32), V((KP, D), f32),
-            V((N, D), bf16), V((N, D), bf16), V((D, N), bf16), V((D, N), bf16),
+            V((N, D), bf16), V((N, D), bf16),
             V((KP, N), f32), V((NT, 8, N), f32), V((NT, 8, N), f32), V((NT, 8, N), f32),
             V((NC, 1, N), f32), V((KP, D), f32), V((KP, 128), f32),
             V((NX, NZ, 128), f32), V((NX - 1, NZ, 128), f32),

time: 81.5 us -> 81.5 us (level)
  no operation moved by 1% of the time
where the time goes in v3:
time: 81.5 us; the launch traced here: 81.4 us
  Pallas kernels  78.1 us (96%)
  local copies, waits for them, and re-layouts  2.02 us (2%)
    pallas_call x1, Pallas kernels, local(): pl.pallas_call(kernel, out_shape=(V((KP, D), f32), V((N,), f32)), in_spec...  78.1 us
    unnamed x1, local copies, waits for them, and re-layouts  2.02 us

profile of v3, /device:TPU:2, one launch (start us, length us, event | category | flops | bytes accessed | tf_op | source)
XLA Modules:
  0.0 81.4 jit_solution(1368582806179367086)
XLA Ops:
  0.6 78.1 %shard_map.41 = (f32[4096,256]{1,0:T(8,128)S(1)}, f32[1024]{0:T(1024)S(1)}) custom-call(f32[1024,256]{1,0:T(8,128)} %x_hbm.1, f32[4096,256]{1,0:T(8,128)} %c_hbm.1), custom_call_target="tpu_custom_call" | custom-call | tf_op jit(solution)/shard_map/pallas_call | solution.py:575
  78.8 2.0 %copy.5 = f32[4096,256]{1,0:T(8,128)} copy(f32[4096,256]{1,0:T(8,128)S(1)} %get-tuple-element.6) | data formatting | bytes 8388608
  80.8 0.6 broadcast_multiply_fusion
